TPU v7x, 512 devices: a whole 4x8x8 slice. The times are simulated.
512 devices in a mesh: snap: 8 (over z), tile: 64 (over x, y, core).
Axes of the slice: x: 4, y: 8, z: 8, core: 2. Of those that a mesh axis runs over, the one named last changes fastest.
Arguments:
- modes: bfloat16 [8192, 256], P(('snap', 'tile')), may hold values from -8 to 8
- targets: bfloat16 [8192, 256], P(('snap', 'tile')), may hold values from -16 to 16
- pairs: int32 [4096, 2], replicated, may hold values from 0 to 256, as said below
- support: int32 [4096, 256], P(('snap', 'tile')), may hold values from 0 to 1, as said below
Outputs:
- coeffs: float32 [4096, 256], P(('snap', 'tile'))
- resid: float32 [4096, 256], P(('snap', 'tile'))
Inputs may be any that keep to these rules, and one draw needn't show every extreme that they name: Rows are distinct unordered pairs; the first entry is below 256; every index below 256 is the first entry of exactly 16 rows. `support`: every target has at least one active term.
All inputs are finite; a program needn't handle non-finite values.
Results may differ from a plain program's by a relative error of at most 0.0036.
Values may be sent and summed in bfloat16 or wider, within the bound.
A program may use at most 64 MiB of HBM per device.

v0:
```python
import jax
import jax.numpy as jnp
from jax import lax
from jax.sharding import PartitionSpec as P

ITERS = 2


def widened(rows_in):
    return jnp.concatenate(
        [rows_in.astype(jnp.float32), jnp.ones((rows_in.shape[0], 1), jnp.float32)], axis=1
    )


def body(modes, targets, pairs, support):
    snap_count = lax.axis_size("snap")
    tile_count = lax.axis_size("tile")
    term_count = pairs.shape[0]
    mode_count = modes.shape[1]
    target_count = targets.shape[1]
    share_rows = term_count // (snap_count * tile_count)
    total_snaps = modes.shape[0] * snap_count * tile_count
    tile_at = lax.axis_index("tile")
    term_grid = jnp.arange(term_count, dtype=jnp.int32).reshape(snap_count, tile_count, share_rows)
    own_terms = lax.dynamic_index_in_dim(term_grid, tile_at, 1, keepdims=False).reshape(-1)
    first_factor = pairs[:, 0]
    second_factor = pairs[:, 1]
    start_sums = (
        jnp.zeros((snap_count * share_rows, term_count), jnp.float32),
        jnp.zeros((snap_count * share_rows, target_count), jnp.float32),
    )
    rows_in = lax.all_gather(modes, "tile", axis=0, tiled=True)
    count_rows = rows_in.shape[0]
    block_rows = max((divisor for divisor in range(1, 513) if count_rows % divisor == 0))

    def inner(totals, block_item):
        block_modes, block_targets = block_item
        extended = widened(block_modes)
        library = (
            jnp.take(extended, first_factor, axis=1) * jnp.take(extended, second_factor, axis=1)
        ).astype(jnp.bfloat16)
        mine = jnp.take(library, own_terms, axis=1)
        gram_sum = totals[0] + lax.dot_general(
            mine, library, (((0,), (0,)), ((), ())), preferred_element_type=jnp.float32
        )
        cross_sum = totals[1] + lax.dot_general(
            mine, block_targets, (((0,), (0,)), ((), ())), preferred_element_type=jnp.float32
        )
        return ((gram_sum, cross_sum), None)

    blocks = (
        rows_in.reshape(count_rows // block_rows, block_rows, mode_count),
        lax.all_gather(targets, "tile", axis=0, tiled=True).reshape(
            count_rows // block_rows, block_rows, target_count
        ),
    )
    results, _ = lax.scan(inner, start_sums, blocks)
    gram_part, cross_part = results
    gram_all, cross_all = lax.psum((gram_part, cross_part), "snap")
    snap_at = lax.axis_index("snap")
    gram_rows = lax.dynamic_slice_in_dim(gram_all, snap_at * share_rows, share_rows, 0)
    cross_rows = lax.dynamic_slice_in_dim(cross_all, snap_at * share_rows, share_rows, 0)
    gram_rows = gram_rows / total_snaps
    cross_rows = cross_rows / total_snaps
    support_mask = support.astype(jnp.float32)

    def energy_of(vector):
        return lax.psum(jnp.sum(vector * vector, axis=0), ("snap", "tile"))

    resid = support_mask * cross_rows
    coeffs = jnp.zeros_like(resid)
    direction = resid
    energy = energy_of(resid)
    for step in range(ITERS):
        product = jnp.dot(
            gram_rows,
            lax.all_gather(direction, ("snap", "tile"), axis=0, tiled=True),
            precision=lax.Precision.HIGHEST,
            preferred_element_type=jnp.float32,
        )
        image = support_mask * product
        step_len = energy / lax.psum(jnp.sum(direction * image, axis=0), ("snap", "tile"))
        coeffs = coeffs + step_len * direction
        resid = resid - step_len * image
        if step + 1 < ITERS:
            fresh = energy_of(resid)
            direction = resid + fresh / energy * direction
            energy = fresh
    return (coeffs, resid)


def solution(mesh):
    return jax.shard_map(
        body,
        mesh=mesh,
        in_specs=(
            P(("snap", "tile"), None),
            P(("snap", "tile"), None),
            P(),
            P(("snap", "tile"), None),
        ),
        out_specs=(P(("snap", "tile"), None), P(("snap", "tile"), None)),
        check_vma=False,
    )
```

profile of v0, /device:TPU:1, one launch (start us, length us, event | category | flops | bytes accessed | tf_op | source)
XLA Modules:
  0.0 834.8 jit_solution(8397565621540414149)
XLA Ops:
  7.2 0.0 all-reduce.5.cloned.1.call-start
  7.2 0.1 reshape.63
  7.3 0.9 fusion.16
  8.2 54.4 %all_gather.12 = bf16[1024,256]{1,0:T(8,128)(2,1)S(1)} all-gather(bf16[16,256]{1,0:T(8,128)(2,1)} %param.8), channel_id=1, replica_groups=mesh['snap'=8,'tile'=64] {'tile'}, dimensions={0}, use_global_device_ids=true | all-gather | bytes 532480 | tf_op jit(solution)/shard_map/all_gather | solution.py:32
  62.6 49.5 %all_gather.13 = bf16[1024,256]{1,0:T(8,128)(2,1)S(1)} all-gather(bf16[16,256]{1,0:T(8,128)(2,1)} %param.9), channel_id=1, replica_groups=mesh['snap'=8,'tile'=64] {'tile'}, dimensions={0}, use_global_device_ids=true | all-gather | bytes 532480 | tf_op jit(solution)/shard_map/all_gather | solution.py:53
  112.0 0.0 copy-start.4
  112.0 101.3 %while.13 = (s32[]{:T(128)}, f32[64,4096]{1,0:T(8,128)S(1)}, f32[64,256]{1,0:T(8,128)S(1)}, s32[64]{0:T(128)S(1)}, bf16[2,512,256]{2,1,0:T(8,128)(2,1)S(1)}, /*i...) while((s32[]{:T(128)}, f32[64,4096]{1,0:T(8,128)S(1)}, ...), condition=%wide.region_1.3_spmd.clone, body=%wide.region_0.2_spmd.clone.sunk | while | flops 294438976 | bytes 63463412 | solution.py:57
  112.1 0.1 copy.9
  112.2 0.1 pad_convert_fusion.2
  112.3 16.9 %gather_fusion.1 = f32[4096,512]{1,0:T(8,128)} fusion(f32[512,257]{0,1:T(8,128)S(1)} %pad_convert_fusion.2, s32[4096]{0:T(1024)S(1)} %get-tuple-element.170), kind=kCustom, calls=%fused_computation.clone.clone.1 | custom fusion | bytes 16793600 | tf_op jit(solution)/shard_map/while/body/eval_jaxpr/jit(_take)/gather | solution.py:40
  129.2 16.9 %gather_fusion = f32[4096,512]{1,0:T(8,128)} fusion(f32[512,257]{0,1:T(8,128)S(1)} %pad_convert_fusion.2, s32[4096]{0:T(1024)S(1)} %get-tuple-element.169), kind=kCustom, calls=%fused_computation.1.clone.clone.1 | custom fusion | bytes 16793600 | tf_op jit(solution)/shard_map/while/body/eval_jaxpr/jit(_take)/gather | solution.py:40
  146.1 9.2 %fusion.28 = bf16[512,4096]{0,1:T(8,128)(2,1)} fusion(f32[4096,512]{1,0:T(8,128)} %gather_fusion, f32[4096,512]{1,0:T(8,128)} %gather_fusion.1, pred[4096]{0:T(1024)(128)(4,1)S(1)} %get-tuple-element.171, pred[4096]{0:T(1024)(128)(4,1)S(1)} %get-tuple-element.172), kind=kLoop, calls=%fused_computation.4.clone.1 | loop fusion | flops 8388608 | bytes 20979712 | tf_op jit(solution)/shard_map/while/body/eval_jaxpr/convert_element_type | solution.py:41
  155.3 3.4 gather_fusion.2
  158.8 3.7 convolution_add_fusion.4
  162.4 0.2 convolution_add_fusion.5
  162.7 0.1 copy.9
  162.9 0.1 pad_convert_fusion.2
  163.0 16.9 %gather_fusion.1 = f32[4096,512]{1,0:T(8,128)} fusion(f32[512,257]{0,1:T(8,128)S(1)} %pad_convert_fusion.2, s32[4096]{0:T(1024)S(1)} %get-tuple-element.170), kind=kCustom, calls=%fused_computation.clone.clone.1 | custom fusion | bytes 16793600 | tf_op jit(solution)/shard_map/while/body/eval_jaxpr/jit(_take)/gather | solution.py:40
  179.8 16.9 %gather_fusion = f32[4096,512]{1,0:T(8,128)} fusion(f32[512,257]{0,1:T(8,128)S(1)} %pad_convert_fusion.2, s32[4096]{0:T(1024)S(1)} %get-tuple-element.169), kind=kCustom, calls=%fused_computation.1.clone.clone.1 | custom fusion | bytes 16793600 | tf_op jit(solution)/shard_map/while/body/eval_jaxpr/jit(_take)/gather | solution.py:40
  196.7 9.2 %fusion.28 = bf16[512,4096]{0,1:T(8,128)(2,1)} fusion(f32[4096,512]{1,0:T(8,128)} %gather_fusion, f32[4096,512]{1,0:T(8,128)} %gather_fusion.1, pred[4096]{0:T(1024)(128)(4,1)S(1)} %get-tuple-element.171, pred[4096]{0:T(1024)(128)(4,1)S(1)} %get-tuple-element.172), kind=kLoop, calls=%fused_computation.4.clone.1 | loop fusion | flops 8388608 | bytes 20979712 | tf_op jit(solution)/shard_map/while/body/eval_jaxpr/convert_element_type | solution.py:41
  205.9 3.4 gather_fusion.2
  209.4 3.7 convolution_add_fusion.4
  213.1 0.2 convolution_add_fusion.5
  213.3 0.0 copy-start
  213.3 0.0 copy-start.1
  213.4 1.0 copy-done
  214.3 0.0 copy-done.1
  214.4 0.0 all-reduce.5.cloned.1.call-update
  214.4 0.0 all-gather.3.cloned.1.call-start
  214.4 77.7 %all-reduce.5.cloned.1.call-done = (f32[64,256]{1,0:T(8,128)}, f32[64,4096]{1,0:T(8,128)}) async-done(((f32[64,256]{1,0:T(8,128)}, f32[64,4096]{1,0:T(8,128)}), (f32[64,256]{1,0:T(8,128)}, f32[64,4096]{1,0:T(8,128)})) %all-reduce.5.cloned.1.call-update) | async-done | bytes 1114128 | tf_op jit(solution)/shard_map/psum | solution.py:59
  292.2 0.0 copy-done.4
  292.2 1.3 multiply_multiply_fusion
  293.5 0.0 copy-start.2
  293.5 0.0 all-gather.3.cloned.1.call-update
  293.5 0.0 all-gather.5.cloned.1.call-start
  293.5 124.9 %all-gather.3.cloned.1.call-done = f32[4096,256]{1,0:T(8,128)} async-done(((f32[8,256]{1,0:T(8,128)}), f32[4096,256]{1,0:T(8,128)}) %all-gather.3.cloned.1.call-update) | async-done | bytes 4194320 | tf_op jit(solution)/shard_map/all_gather | solution.py:77
  418.5 3.9 multiply_reduce_fusion.2
  422.4 96.1 %all-reduce.1 = (f32[256]{0:T(256)S(1)}, f32[256]{0:T(256)S(1)}) all-reduce(f32[256]{0:T(256)S(1)} %get-tuple-element.84, f32[256]{0:T(256)S(1)} %get-tuple-element.83), channel_id=1, replica_groups=mesh['snap'=8,'tile'=64] {'snap','tile'}, use_global_device_ids=true, to_apply=%region_4.6 | all-reduce | flops 512 | bytes 4096 | tf_op jit(solution)/shard_map/psum | solution.py:68
  518.5 0.0 copy-done.2
  518.6 93.8 %psum.46 = f32[256]{0:T(256)S(1)} all-reduce(f32[256]{0:T(256)S(1)} %multiply_reduce_fusion.1), channel_id=1, replica_groups=mesh['snap'=8,'tile'=64] {'snap','tile'}, use_global_device_ids=true, to_apply=%region_9.11 | all-reduce | flops 256 | bytes 2048 | tf_op jit(solution)/shard_map/psum | solution.py:68
  612.4 0.6 multiply_add_fusion.1
  613.0 0.0 copy-start.3
  613.0 0.0 all-gather.5.cloned.1.call-update
  613.0 114.6 %all-gather.5.cloned.1.call-done = f32[4096,256]{1,0:T(8,128)} async-done(((f32[8,256]{1,0:T(8,128)}), f32[4096,256]{1,0:T(8,128)}) %all-gather.5.cloned.1.call-update) | async-done | bytes 4194320 | tf_op jit(solution)/shard_map/all_gather | solution.py:77
  727.6 3.9 multiply_reduce_fusion
  731.5 96.2 %psum.47 = f32[256]{0:T(256)S(1)} all-reduce(f32[256]{0:T(256)S(1)} %get-tuple-element.114), channel_id=1, replica_groups=mesh['snap'=8,'tile'=64] {'snap','tile'}, use_global_device_ids=true, to_apply=%region_11.13 | all-reduce | flops 256 | bytes 2048 | tf_op jit(solution)/shard_map/psum | solution.py:82
  827.7 0.0 copy-done.3
  827.7 0.6 multiply_subtract_fusion
  (19 shorter events, 0.2 us)
Async XLA Ops:
  7.2 285.0 %all-reduce.5.cloned.1.call-start = ((), (), s32[]{:S(2)}) async-start(), calls=%async_computation.2 | async-start | bytes 2228224 | tf_op jit(solution)/shard_map/psum | solution.py:59
  112.0 180.1 %copy-start.4 = (s32[8,256]{1,0:T(8,128)S(1)}, s32[8,256]{1,0:T(8,128)}, u32[]{:S(2)}) copy-start(s32[8,256]{1,0:T(8,128)} %param.11) | copy-start | bytes 24580
  213.3 1.0 copy-start
  213.3 1.0 copy-start.1
  214.4 204.1 %all-gather.3.cloned.1.call-start = ((), (), s32[]{:S(2)}) async-start(), calls=%async_computation | async-start | bytes 4202496 | tf_op jit(solution)/shard_map/all_gather | solution.py:77
  293.5 225.1 %copy-start.2 = (f32[8,256]{1,0:T(8,128)S(1)}, f32[8,256]{1,0:T(8,128)}, u32[]{:S(2)}) copy-start(f32[8,256]{1,0:T(8,128)} %multiply_multiply_fusion) | copy-start | bytes 24580
  293.5 434.1 %all-gather.5.cloned.1.call-start = ((), (), s32[]{:S(2)}) async-start(), calls=%async_computation.1 | async-start | bytes 4202496 | tf_op jit(solution)/shard_map/all_gather | solution.py:77
  613.0 214.7 %copy-start.3 = (f32[8,256]{1,0:T(8,128)S(1)}, f32[8,256]{1,0:T(8,128)}, u32[]{:S(2)}) copy-start(f32[8,256]{1,0:T(8,128)} %multiply_add_fusion.1) | copy-start | bytes 24580
Sparse Core Ops, SparseCore 0:
  214.5 77.6 all-reduce.4
  297.6 120.7 all-gather.2
  613.1 114.4 all-gather.4
where the time goes:
time: 835 us
  blocking collectives  390 us (47%)
  waiting for transfers between devices  317 us (38%)
  local copies, waits for them, and re-layouts  76.7 us (9%)
  other arithmetic  21.2 us (3%)
  matrix products  15.7 us (2%)
  between operations  13.8 us (2%)
    all_gather x2, waiting for transfers between devices, body(): lax.all_gather(direction, ('snap', 'tile'), axis=0, tiled=True)  239 us
    psum x2, blocking collectives, energy_of(): return lax.psum(jnp.sum(vector * vector, axis=0), ('snap', 'tile'))  190 us
    psum x1, blocking collectives, body(): lax.psum(jnp.sum(direction * image, axis=0), ('snap', 'tile'))  96.2 us
    psum x1, waiting for transfers between devices, body(): gram_all, cross_all = lax.psum((gram_part, cross_part), 'snap')  77.7 us
    all_gather x1, blocking collectives, body(): rows_in = lax.all_gather(modes, 'tile', axis=0, tiled=True)  54.4 us
    all_gather x1, blocking collectives, body(): lax.all_gather(targets, 'tile', axis=0, tiled=True)  49.5 us
    gather x2, local copies, waits for them, and re-layouts, inner(): jnp.take(extended, first_factor, axis=1)  33.8 us
    gather x2, local copies, waits for them, and re-layouts, inner(): jnp.take(extended, second_factor, axis=1)  33.7 us
  transfers between devices with their start and end apart: 3, of which 3 were waited for; matrix products, arithmetic and copies ran while one was open for 0% of the time, Pallas kernels for 0%

commit v1 on v0

--- a/solution.py
+++ b/solution.py
@@ -79,7 +79,7 @@
             preferred_element_type=jnp.float32,
         )
         image = support_mask * product
-        step_len = energy / lax.psum(jnp.sum(direction * image, axis=0), ("snap", "tile"))
+        step_len = energy / lax.psum(lax.psum(jnp.sum(direction * image, axis=0), "tile"), "snap")
         coeffs = coeffs + step_len * direction
         resid = resid - step_len * image
         if step + 1 < ITERS:

time: 835 us -> 1020 us (1.22)
  blocking collectives: 390 us -> 571 us
    psum x1 -> x4, blocking collectives: 96.2 us -> 273 us  [the longest x2 247 us: body(): lax.psum(jnp.sum(direction * image, axis=0), 'tile')]
where the time goes in v1:
time: 1020 us; the launch traced here: 1010 us
  blocking collectives  571 us (56%)
  waiting for transfers between devices  315 us (31%)
  local copies, waits for them, and re-layouts  76.3 us (7%)
  other arithmetic  21.2 us (2%)
  matrix products  15.7 us (2%)
  between operations  13.8 us (1%)
    psum x2, blocking collectives, body(): lax.psum(jnp.sum(direction * image, axis=0), 'tile')  247 us
    all_gather x2, waiting for transfers between devices, body(): lax.all_gather(direction, ('snap', 'tile'), axis=0, tiled=True)  237 us
    psum x2, blocking collectives, energy_of(): return lax.psum(jnp.sum(vector * vector, axis=0), ('snap', 'tile'))  195 us
    psum x1, waiting for transfers between devices, body(): gram_all, cross_all = lax.psum((gram_part, cross_part), 'snap')  77.7 us
    all_gather x1, blocking collectives, body(): rows_in = lax.all_gather(modes, 'tile', axis=0, tiled=True)  54.4 us
    all_gather x1, blocking collectives, body(): lax.all_gather(targets, 'tile', axis=0, tiled=True)  49.5 us
    gather x2, local copies, waits for them, and re-layouts, inner(): jnp.take(extended, first_factor, axis=1)  33.6 us
    gather x2, local copies, waits for them, and re-layouts, inner(): jnp.take(extended, second_factor, axis=1)  33.6 us
  transfers between devices with their start and end apart: 3, of which 3 were waited for; matrix products, arithmetic and copies ran while one was open for 0% of the time, Pallas kernels for 0%

profile of v1, /device:TPU:1, one launch (start us, length us, event | category | flops | bytes accessed | tf_op | source)
XLA Modules:
  0.0 1013.8 jit_solution(16876073575547507727)
XLA Ops:
  7.2 0.0 all-reduce.4.cloned.1.call-start
  7.2 0.1 reshape.63
  7.3 0.9 fusion.16
  8.2 54.4 %all_gather.12 = bf16[1024,256]{1,0:T(8,128)(2,1)S(1)} all-gather(bf16[16,256]{1,0:T(8,128)(2,1)} %param.8), channel_id=1, replica_groups=mesh['snap'=8,'tile'=64] {'tile'}, dimensions={0}, use_global_device_ids=true | all-gather | bytes 532480 | tf_op jit(solution)/shard_map/all_gather | solution.py:32
  62.6 49.5 %all_gather.13 = bf16[1024,256]{1,0:T(8,128)(2,1)S(1)} all-gather(bf16[16,256]{1,0:T(8,128)(2,1)} %param.9), channel_id=1, replica_groups=mesh['snap'=8,'tile'=64] {'tile'}, dimensions={0}, use_global_device_ids=true | all-gather | bytes 532480 | tf_op jit(solution)/shard_map/all_gather | solution.py:53
  112.0 0.0 copy-start.4
  112.0 101.0 %while.13 = (s32[]{:T(128)}, f32[64,4096]{1,0:T(8,128)S(1)}, f32[64,256]{1,0:T(8,128)S(1)}, s32[64]{0:T(128)S(1)}, bf16[2,512,256]{2,1,0:T(8,128)(2,1)S(1)}, /*i...) while((s32[]{:T(128)}, f32[64,4096]{1,0:T(8,128)S(1)}, ...), condition=%wide.region_1.3_spmd.clone, body=%wide.region_0.2_spmd.clone.sunk | while | flops 294438976 | bytes 63463412 | solution.py:57
  112.1 0.1 copy.9
  112.2 0.1 pad_convert_fusion.2
  112.3 16.8 %gather_fusion.1 = f32[4096,512]{1,0:T(8,128)} fusion(f32[512,257]{0,1:T(8,128)S(1)} %pad_convert_fusion.2, s32[4096]{0:T(1024)S(1)} %get-tuple-element.168), kind=kCustom, calls=%fused_computation.clone.clone.1 | custom fusion | bytes 16793600 | tf_op jit(solution)/shard_map/while/body/eval_jaxpr/jit(_take)/gather | solution.py:40
  129.1 16.8 %gather_fusion = f32[4096,512]{1,0:T(8,128)} fusion(f32[512,257]{0,1:T(8,128)S(1)} %pad_convert_fusion.2, s32[4096]{0:T(1024)S(1)} %get-tuple-element.167), kind=kCustom, calls=%fused_computation.1.clone.clone.1 | custom fusion | bytes 16793600 | tf_op jit(solution)/shard_map/while/body/eval_jaxpr/jit(_take)/gather | solution.py:40
  145.9 9.2 fusion.28
  155.1 3.4 gather_fusion.2
  158.6 3.7 convolution_add_fusion.4
  162.3 0.2 convolution_add_fusion.5
  162.6 0.1 copy.9
  162.7 0.1 pad_convert_fusion.2
  162.8 16.8 %gather_fusion.1 = f32[4096,512]{1,0:T(8,128)} fusion(f32[512,257]{0,1:T(8,128)S(1)} %pad_convert_fusion.2, s32[4096]{0:T(1024)S(1)} %get-tuple-element.168), kind=kCustom, calls=%fused_computation.clone.clone.1 | custom fusion | bytes 16793600 | tf_op jit(solution)/shard_map/while/body/eval_jaxpr/jit(_take)/gather | solution.py:40
  179.6 16.8 %gather_fusion = f32[4096,512]{1,0:T(8,128)} fusion(f32[512,257]{0,1:T(8,128)S(1)} %pad_convert_fusion.2, s32[4096]{0:T(1024)S(1)} %get-tuple-element.167), kind=kCustom, calls=%fused_computation.1.clone.clone.1 | custom fusion | bytes 16793600 | tf_op jit(solution)/shard_map/while/body/eval_jaxpr/jit(_take)/gather | solution.py:40
  196.4 9.2 fusion.28
  205.6 3.4 gather_fusion.2
  209.1 3.7 convolution_add_fusion.4
  212.8 0.2 convolution_add_fusion.5
  213.0 0.0 copy-start
  213.0 0.0 copy-start.1
  213.0 1.0 copy-done
  214.0 0.0 copy-done.1
  214.0 0.0 all-reduce.4.cloned.1.call-update
  214.1 0.0 all-gather.3.cloned.1.call-start
  214.1 77.7 %all-reduce.4.cloned.1.call-done = (f32[64,256]{1,0:T(8,128)}, f32[64,4096]{1,0:T(8,128)}) async-done(((f32[64,256]{1,0:T(8,128)}, f32[64,4096]{1,0:T(8,128)}), (f32[64,256]{1,0:T(8,128)}, f32[64,4096]{1,0:T(8,128)})) %all-reduce.4.cloned.1.call-update) | async-done | bytes 1114128 | tf_op jit(solution)/shard_map/psum | solution.py:59
  291.8 0.0 copy-done.4
  291.8 1.3 multiply_multiply_fusion
  293.1 0.0 copy-start.2
  293.1 0.0 all-gather.3.cloned.1.call-update
  293.2 0.0 all-gather.5.cloned.1.call-start
  293.2 124.9 %all-gather.3.cloned.1.call-done = f32[4096,256]{1,0:T(8,128)} async-done(((f32[8,256]{1,0:T(8,128)}), f32[4096,256]{1,0:T(8,128)}) %all-gather.3.cloned.1.call-update) | async-done | bytes 4194320 | tf_op jit(solution)/shard_map/all_gather | solution.py:77
  418.1 3.9 multiply_reduce_fusion.2
  422.1 123.7 %psum.59 = f32[256]{0:T(256)S(1)} all-reduce(f32[256]{0:T(256)S(1)} %get-tuple-element.83), channel_id=1, replica_groups=mesh['snap'=8,'tile'=64] {'tile'}, use_global_device_ids=true, to_apply=%region_7.9 | all-reduce | flops 256 | bytes 2048 | tf_op jit(solution)/shard_map/psum | solution.py:82
  545.7 12.7 %psum.60 = f32[256]{0:T(256)S(1)} all-reduce(f32[256]{0:T(256)S(1)} %psum.59), channel_id=1, replica_groups=mesh['snap'=8,'tile'=64] {'snap'}, use_global_device_ids=true, to_apply=%region_8.10 | all-reduce | flops 256 | bytes 2048 | tf_op jit(solution)/shard_map/psum | solution.py:82
  558.4 99.0 %psum.57 = f32[256]{0:T(256)S(1)} all-reduce(f32[256]{0:T(256)S(1)} %get-tuple-element.84), channel_id=1, replica_groups=mesh['snap'=8,'tile'=64] {'snap','tile'}, use_global_device_ids=true, to_apply=%region_4.6 | all-reduce | flops 256 | bytes 2048 | tf_op jit(solution)/shard_map/psum | solution.py:68
  657.4 0.0 copy-done.2
  657.5 95.7 %psum.61 = f32[256]{0:T(256)S(1)} all-reduce(f32[256]{0:T(256)S(1)} %multiply_reduce_fusion.1), channel_id=1, replica_groups=mesh['snap'=8,'tile'=64] {'snap','tile'}, use_global_device_ids=true, to_apply=%region_10.12 | all-reduce | flops 256 | bytes 2048 | tf_op jit(solution)/shard_map/psum | solution.py:68
  753.2 0.6 multiply_add_fusion.1
  753.8 0.0 copy-start.3
  753.8 0.0 all-gather.5.cloned.1.call-update
  753.8 112.5 %all-gather.5.cloned.1.call-done = f32[4096,256]{1,0:T(8,128)} async-done(((f32[8,256]{1,0:T(8,128)}), f32[4096,256]{1,0:T(8,128)}) %all-gather.5.cloned.1.call-update) | async-done | bytes 4194320 | tf_op jit(solution)/shard_map/all_gather | solution.py:77
  866.3 3.9 multiply_reduce_fusion
  870.3 123.7 %psum.62 = f32[256]{0:T(256)S(1)} all-reduce(f32[256]{0:T(256)S(1)} %get-tuple-element.112), channel_id=1, replica_groups=mesh['snap'=8,'tile'=64] {'tile'}, use_global_device_ids=true, to_apply=%region_12.14 | all-reduce | flops 256 | bytes 2048 | tf_op jit(solution)/shard_map/psum | solution.py:82
  993.9 12.7 %psum.63 = f32[256]{0:T(256)S(1)} all-reduce(f32[256]{0:T(256)S(1)} %psum.62), channel_id=1, replica_groups=mesh['snap'=8,'tile'=64] {'snap'}, use_global_device_ids=true, to_apply=%region_13.15 | all-reduce | flops 256 | bytes 2048 | tf_op jit(solution)/shard_map/psum | solution.py:82
  1006.6 0.0 copy-done.3
  1006.6 0.6 multiply_subtract_fusion
  (19 shorter events, 0.2 us)
Async XLA Ops:
  7.2 284.7 %all-reduce.4.cloned.1.call-start = ((), (), s32[]{:S(2)}) async-start(), calls=%async_computation.2 | async-start | bytes 2228224 | tf_op jit(solution)/shard_map/psum | solution.py:59
  112.0 179.8 %copy-start.4 = (s32[8,256]{1,0:T(8,128)S(1)}, s32[8,256]{1,0:T(8,128)}, u32[]{:S(2)}) copy-start(s32[8,256]{1,0:T(8,128)} %param.11) | copy-start | bytes 24580
  213.0 1.0 copy-start
  213.0 1.0 copy-start.1
  214.1 204.1 %all-gather.3.cloned.1.call-start = ((), (), s32[]{:S(2)}) async-start(), calls=%async_computation | async-start | bytes 4202496 | tf_op jit(solution)/shard_map/all_gather | solution.py:77
  293.1 364.3 %copy-start.2 = (f32[8,256]{1,0:T(8,128)S(1)}, f32[8,256]{1,0:T(8,128)}, u32[]{:S(2)}) copy-start(f32[8,256]{1,0:T(8,128)} %multiply_multiply_fusion) | copy-start | bytes 24580
  293.2 573.2 %all-gather.5.cloned.1.call-start = ((), (), s32[]{:S(2)}) async-start(), calls=%async_computation.1 | async-start | bytes 4202496 | tf_op jit(solution)/shard_map/all_gather | solution.py:77
  753.8 252.8 %copy-start.3 = (f32[8,256]{1,0:T(8,128)S(1)}, f32[8,256]{1,0:T(8,128)}, u32[]{:S(2)}) copy-start(f32[8,256]{1,0:T(8,128)} %multiply_add_fusion.1) | copy-start | bytes 24580
Sparse Core Ops, SparseCore 0:
  214.2 77.6 all-reduce.3
  297.3 120.7 all-gather.2
  753.9 112.3 all-gather.4
